TPU v7x, 128 devices: a whole 4x4x4 slice. The times are simulated.
128 devices in a mesh: chain: 8 (over y, core), bond: 16 (over z, x).
Axes of the slice: x: 4, y: 4, z: 4, core: 2. Of those that a mesh axis runs over, the one named last changes fastest.
Arguments:
- wavefunction: bfloat16 [8, 16, 512, 512], P('chain', 'bond'), may hold values from -6 to 6
- left_env: bfloat16 [8, 16, 12, 512, 512], P('chain', 'bond'), may hold values from -0.25 to 0.25
- right_env: bfloat16 [8, 16, 12, 512, 512], P('chain', 'bond'), may hold values from -0.25 to 0.25
- source: int32 [8, 16, 12], P('chain', 'bond'), may hold values from 0 to 15
- block_sizes: int32 [8, 16], P('chain', 'bond'), may hold values from 128 to 512, as said below
- davidson_mix: float32 [8, 3, 3], P('chain'), may hold values from -0.5 to 0.5
- ritz_weights: float32 [8, 4], P('chain'), may hold values from 0.25 to 1
Outputs:
- updated: bfloat16 [8, 16, 512, 512], P('chain', 'bond')
- handed_env: bfloat16 [8, 16, 12, 512, 512], P('chain', 'bond')
Inputs may be any that keep to these rules, and one draw needn't show every extreme that they name: `block_sizes`: in every section some sector's block is full.
All inputs are finite; a program needn't handle non-finite values.
Results may differ from a plain program's by a relative error of at most 0.025.
Values may be sent and summed in bfloat16 or wider, within the bound.
A program may use at most 128 MiB of HBM per device.

v0:
```python
import math

import jax
import jax.numpy as jnp
from jax import lax
from jax.experimental import pallas as pl
from jax.experimental.pallas import tpu as pltpu
from jax.sharding import PartitionSpec as P

PRODUCTS = 3
EPSILON = 1e-06
MESH = pl.DeviceIdType.MESH
RING = 4
LANES = 128
F32 = jnp.float32
BF16 = jnp.bfloat16

ORDER = (
    (("E", 1, 0), ("E", 1, 1), ("E", 2, 0), ("E", 1, 2), ("E", 3, 0), ("E", 2, 1), ("E", 1, 3), ("E", 4, 0))
    + (("C", 0, 0), ("E", 3, 1), ("C", 0, 1), ("E", 2, 2), ("C", 0, 2), ("E", 4, 1), ("C", 0, 3), ("S", 0))
    + (("E", 3, 2), ("C", 1, 0), ("C", 1, 1), ("E", 2, 3), ("C", 1, 2), ("C", 1, 3), ("S", 1), ("E", 4, 2))
    + (("C", 2, 0), ("E", 3, 3), ("C", 2, 1), ("C", 2, 2), ("C", 2, 3), ("S", 2), ("E", 4, 3))
)
EARLY = (("E", 1, 0), ("E", 1, 1), ("E", 2, 0), ("E", 1, 2))

TURN = ("E", 4, 0)


class Gather:
    def __init__(self, parts, send, recv, z, x, width):
        self.parts, self.send, self.recv = parts, send, recv
        self.z, self.x = z, x
        self.me = z * RING + x
        self.half = width // 2
        self.quarter = width // 4

    def sector(self, path, first, second):
        a, b = (self.x, self.z) if path == 0 else (self.z, self.x)
        a = lax.rem(a + (first + RING), RING)
        b = lax.rem(b + (second + RING), RING)
        return b * RING + a if path == 0 else a * RING + b

    def copy(self, part, path, sector, offset, rows, device, slot):
        ref = self.parts[part].at[sector, pl.ds(path * self.half + offset, rows), :]
        return pltpu.make_async_remote_copy(
            src_ref=ref,
            dst_ref=ref,
            send_sem=self.send.at[part],
            recv_sem=self.recv.at[part, path, slot],
            device_id={"bond": device},
            device_id_type=MESH,
        )

    OFFSETS = (0, 1, -1, 2)

    def own_first(self, part, path):
        for slot, way in ((0, 1), (1, -1)):
            self.copy(part, path, self.me, 0, self.half, self.sector(path, way, 0), slot).start()

    def own_second(self, part, path, which):
        sector = self.sector(path, self.OFFSETS[which], 0)
        for side, way in ((0, 1), (1, -1)):
            slot = 4 + 4 * which + side
            self.copy(part, path, sector, 0, self.half, self.sector(path, 0, way), slot).start()

    def pass_first(self, part, path, side):
        way = 1 if side == 0 else -1
        sector = self.sector(path, -way, 0)
        self.copy(part, path, sector, 0, self.half, self.me, side).wait_recv()
        target = self.sector(path, way, 0)
        self.copy(part, path, sector, self.quarter * side, self.quarter, target, 2 + side).start()

    def end_first(self, part, path):
        sector = self.sector(path, 2, 0)
        for side in (0, 1):
            self.copy(part, path, sector, self.quarter * side, self.quarter, self.me, 2 + side).wait_recv()

    def pass_second(self, part, path, which, side):
        way = 1 if side == 0 else -1
        sector = self.sector(path, self.OFFSETS[which], -way)
        slot = 4 + 4 * which + side
        self.copy(part, path, sector, 0, self.half, self.me, slot).wait_recv()
        target = self.sector(path, 0, way)
        self.copy(part, path, sector, self.quarter * side, self.quarter, target, slot + 2).start()

    def end_second(self, part, path, which):
        sector = self.sector(path, self.OFFSETS[which], 2)
        for side in (0, 1):
            slot = 4 + 4 * which + 2 + side
            self.copy(part, path, sector, self.quarter * side, self.quarter, self.me, slot).wait_recv()

    def stage(self, number, part):
        if number == 0:
            for path in (0, 1):
                self.own_first(part, path)
            for path in (0, 1):
                self.own_second(part, path, 0)
        elif number == 1:
            for side in (0, 1):
                for path in (0, 1):
                    self.pass_first(part, path, side)
                    self.own_second(part, path, 2 if side == 0 else 1)
            for side in (0, 1):
                for path in (0, 1):
                    self.pass_second(part, path, 0, side)
        elif number == 2:
            for path in (0, 1):
                self.end_first(part, path)
                self.own_second(part, path, 3)
            for which in (1, 2):
                for side in (0, 1):
                    for path in (0, 1):
                        self.pass_second(part, path, which, side)
        elif number == 3:
            for side in (0, 1):
                for path in (0, 1):
                    self.pass_second(part, path, 3, side)
        else:
            for path in (0, 1):
                for which in range(4):
                    self.end_second(part, path, which)

    def sent(self, part):
        ref = self.parts[part].at[pl.ds(0, RING * RING - 1)]
        pltpu.make_async_remote_copy(
            src_ref=ref,
            dst_ref=ref,
            send_sem=self.send.at[part],
            recv_sem=self.recv.at[part, 0, 0],
            device_id={"bond": self.me},
            device_id_type=MESH,
        ).wait_send()


def kernel(
    wave_ref,
    left_ref,
    right_ref,
    source_ref,
    sizes_ref,
    mixing_hbm,
    weights_ref,
    updated_ref,
    handed_ref,
    *scratch,
):
    terms, width = left_ref.shape[2], left_ref.shape[3]
    count = width // LANES
    group = terms // 4
    parts = (scratch[:count], scratch[count : 2 * count])
    (
        left,
        right,
        turned,
        landed_left,
        half,
        total,
        own,
        combined,
        handed_vector,
        flipped,
        norm_own,
        norm_first,
        norm_row,
        norm_second,
        norm_all,
        norm_landed,
        source_tile,
        source_landed,
        source_before,
        mixing_ref,
        load_sem,
        send_sem,
        recv_sem,
        norm_send,
        norm_recv,
        chain_send,
        chain_recv,
        local_sem,
        out_sem,
        turn_sem,
    ) = scratch[2 * count :]
    chain = lax.axis_index("chain")
    bond = lax.axis_index("bond")
    chains = lax.axis_size("chain")
    z, x = lax.div(bond, RING), lax.rem(bond, RING)
    after = lax.rem(chain + 1, chains)
    before = lax.rem(chain + chains - 1, chains)
    entries = float(RING * RING * width * width)

    load_left = pltpu.make_async_copy(left_ref.at[0, 0], left, load_sem.at[0])
    load_right = pltpu.make_async_copy(right_ref.at[0, 0], right, load_sem.at[1])
    load_left.start()
    load_right.start()
    load_mixing = pltpu.make_async_copy(mixing_hbm, mixing_ref, load_sem.at[2])
    load_mixing.start()

    def along_x(by):
        return z * RING + lax.rem(x + by, RING)

    def along_z(by):
        return lax.rem(z + by, RING) * RING + x

    barrier = pltpu.get_barrier_semaphore()
    for by in range(1, RING):
        for device in (along_x(by), along_z(by)):
            pl.semaphore_signal(barrier, inc=1, device_id={"bond": device}, device_id_type=MESH)
    for device in (after, before):
        pl.semaphore_signal(barrier, inc=1, device_id={"chain": device}, device_id_type=MESH)

    size = sizes_ref[0, 0]
    row_live = lax.broadcasted_iota(jnp.int32, (width, LANES), 0) < size

    def masked(value, part):
        column = lax.broadcasted_iota(jnp.int32, (width, LANES), 1) + part * LANES
        return jnp.where(row_live & (column < size), value, 0.0)

    def columns(part):
        return pl.ds(part * LANES, LANES)

    def tile_sum(value):
        return jnp.sum((value * value).reshape(width // 8, 8, LANES), axis=0)

    gathers = [
        Gather(parts[number % 2], send_sem.at[number % 2], recv_sem.at[number % 2], z, x, width)
        for number in range(PRODUCTS + 1)
    ]

    def to_chain(src, dst, slot):
        return pltpu.make_async_remote_copy(
            src_ref=src,
            dst_ref=dst,
            send_sem=chain_send.at[slot],
            recv_sem=chain_recv.at[slot],
            device_id={"chain": after},
            device_id_type=MESH,
        )

    def norm_copy(number, phase, by):
        return pltpu.make_async_remote_copy(
            src_ref=(norm_own if phase == 0 else norm_row).at[number],
            dst_ref=(norm_first if phase == 0 else norm_second).at[number, by - 1],
            send_sem=norm_send.at[number, phase, by - 1],
            recv_sem=norm_recv.at[number, phase, by - 1],
            device_id={"bond": along_x(by) if phase == 0 else along_z(by)},
            device_id_type=MESH,
        )

    def norm_start(number, tile):
        norm_own[number] = tile
        for by in range(1, RING):
            norm_copy(number, 0, by).start()

    def norm_middle(number):
        for by in range(1, RING):
            norm_copy(number, 0, by).wait_recv()
        norm_row[number] = norm_own[number] + norm_first[number, 0] + norm_first[number, 1] + norm_first[number, 2]
        for by in range(1, RING):
            norm_copy(number, 1, by).start()

    def scale_of(tile):
        summed = jnp.sum(jnp.sum(tile, axis=0, keepdims=True), axis=1, keepdims=True)
        return lax.rsqrt(summed / entries + EPSILON)

    def norm_end(number):
        for by in range(1, RING):
            norm_copy(number, 1, by).wait_recv()
        norm_all[number] = (
            norm_row[number] + norm_second[number, 0] + norm_second[number, 1] + norm_second[number, 2]
        )
        return scale_of(norm_all[number])

    def place(number, part, value):
        own[number, part] = value
        parts[number % 2][part][bond] = value

    values = []
    squares = jnp.zeros((8, LANES), F32)
    for part in range(count):
        value = masked(wave_ref[0, 0, :, columns(part)].astype(F32), part)
        squares = squares + tile_sum(value)
        place(0, part, value.astype(BF16))
    lane = lax.broadcasted_iota(jnp.int32, (8, LANES), 1)
    tile = jnp.zeros((8, LANES), jnp.int32)
    for term in range(terms):
        tile = jnp.where(lane == term, source_ref[0, 0, term], tile)
    source_tile[...] = tile

    pl.semaphore_wait(barrier, 2 * (RING - 1) + 2)
    odd = lax.rem(chain, 2) == 1

    @pl.when(odd)
    def _():
        pl.semaphore_wait(turn_sem, 1)

    gathers[0].stage(0, 0)
    norm_start(0, squares)
    for part in range(1, count):
        gathers[0].stage(0, part)
    send_source = to_chain(source_tile, source_landed, 0)
    send_source.start()
    send_left = to_chain(left_ref.at[0, 0], landed_left, 1)
    send_left.start()

    def turn(number):
        def step(term, carry):
            for part in range(count):
                rows = pl.ds(pl.multiple_of(term * LANES, LANES), LANES)
                turned[part, rows, :] = jnp.transpose(right[term, :, columns(part)])
            return carry

        lax.fori_loop(number * group, (number + 1) * group, step, 0)

    def halves(number, part, which):
        held = parts[number % 2][part]

        def step(term, carry):
            block = held[source_ref[0, 0, term]]
            product = jnp.dot(left[term], block, preferred_element_type=F32)
            half[:, pl.ds(pl.multiple_of(term * LANES, LANES), LANES)] = product.astype(BF16)
            return carry

        lax.fori_loop(which * group, (which + 1) * group, step, 0, unroll=part == count - 1)

    def gather_sum(part, side):
        wide = pl.ds(side * (width // 2), width // 2)
        product = jnp.dot(half[...], turned[part, :, wide], preferred_element_type=F32)
        if part == 0:
            total[:, wide] = product
        else:
            total[:, wide] += product

    scales = []
    for number in range(PRODUCTS):
        here = gathers[number]
        for item in ORDER:
            if item[0] == "E":
                here.stage(*item[1:])
                if item == EARLY[0]:
                    norm_middle(number)
                if number == 0 and item == TURN:

                    @pl.when(jnp.logical_not(odd))
                    def _():
                        pl.semaphore_signal(turn_sem, inc=1, device_id={"chain": after}, device_id_type=MESH)

                if number == 0 and item in EARLY:
                    if item == EARLY[0]:
                        load_right.wait()
                    turn(EARLY.index(item))
                if number == 0 and item == ("E", 4, 0):
                    load_left.wait()
                    load_mixing.wait()
            elif item[0] == "C":
                halves(number, *item[1:])
            else:
                for side in (0, 1):
                    gather_sum(item[1], side)
        scales.append(norm_end(number))
        for which in range(4):
            halves(number, count - 1, which)
        for part in range(count):
            here.sent(part)
        squares = jnp.zeros((8, LANES), F32)
        for side in (0, 1):
            gather_sum(count - 1, side)
            for part in range(side * count // 2, (side + 1) * count // 2):
                value = scales[number] * masked(total[:, columns(part)], part)
                for other in range(number + 1):
                    factor = mixing_ref[0, number : number + 1, other : other + 1] * scales[other]
                    value = value - factor * own[other, part].astype(F32)
                squares = squares + tile_sum(value)
                if number + 1 < PRODUCTS:
                    place(number + 1, part, value.astype(BF16))
                    gathers[number + 1].stage(0, part)
                else:
                    combined[:, columns(part)] = value
        norm_start(number + 1, squares)

    norm_middle(PRODUCTS)
    last = norm_end(PRODUCTS)
    squares = jnp.zeros((8, LANES), F32)
    for part in range(count):
        value = (weights_ref[0, PRODUCTS] * last) * combined[:, columns(part)]
        for other in range(PRODUCTS):
            value = value + (weights_ref[0, other] * scales[other]) * own[other, part].astype(F32)
        combined[:, columns(part)] = value
        own[PRODUCTS, part] = value.astype(BF16)
        to_chain(own.at[PRODUCTS, part], handed_vector.at[part], 3 + part).start()
        squares = squares + tile_sum(value)
    norm_start(PRODUCTS + 1, squares)

    here = gathers[PRODUCTS]
    for part in range(count):
        to_chain(own.at[PRODUCTS, part], handed_vector.at[part], 3 + part).wait_recv()
        parts[PRODUCTS % 2][part][bond] = handed_vector[part]
        here.stage(0, part)
    norm_middle(PRODUCTS + 1)
    send_source.wait_recv()
    fetch_source = pltpu.make_async_copy(source_landed, source_before, local_sem)
    fetch_source.start()
    for part in range(count):
        flipped[pl.ds(part * LANES, LANES), :] = jnp.transpose(handed_vector[part])
    fetch_source.wait()
    send_left.wait_recv()

    def grow_half(which):
        def step(term, carry):
            product = jnp.dot(flipped[...], landed_left[term], preferred_element_type=F32)
            right[term] = product.astype(BF16)
            return carry

        lax.fori_loop(which * group, (which + 1) * group, step, 0)

    def out_copy(part):
        return pltpu.make_async_copy(
            left.at[:, :, columns(part)], handed_ref.at[0, 0, :, :, columns(part)], out_sem.at[part]
        )

    def grow(part, which, factor):
        held = parts[PRODUCTS % 2][part]

        def step(term, carry):
            block = held[source_before[0, term]]
            product = jnp.dot(right[term], block, preferred_element_type=F32)
            left[term, :, columns(part)] = (product * factor).astype(BF16)
            return carry

        lax.fori_loop(which * group, (which + 1) * group, step, 0, unroll=part == count - 1)

    factor = None
    for item in ORDER:
        if item[0] == "E":
            here.stage(*item[1:])
            if item in EARLY:
                grow_half(EARLY.index(item))
            if item == EARLY[0]:
                scale = norm_end(PRODUCTS + 1)
                send_norm = to_chain(norm_all.at[PRODUCTS + 1], norm_landed, 2)
                send_norm.start()
                for column in range(count):
                    updated_ref[0, 0, :, columns(column)] = (scale * combined[:, columns(column)]).astype(BF16)
            if item == ("E", 3, 0):
                send_norm.wait_recv()
                scale = scale_of(norm_landed[...])
                factor = scale * scale * (1.0 / math.sqrt(width))
                factor = jnp.where(chain > 0, factor, jnp.zeros_like(factor))
        elif item[0] == "C":
            grow(*item[1:], factor)
        else:
            out_copy(item[1]).start()
    for which in range(4):
        grow(count - 1, which, factor)
    out_copy(count - 1).start()
    for part in range(count):
        here.sent(part)
    for number in range(PRODUCTS + 2):
        for phase in (0, 1):
            for by in range(1, RING):
                norm_copy(number, phase, by).wait_send()
    send_source.wait_send()
    send_left.wait_send()
    send_norm.wait_send()
    for part in range(count):
        to_chain(own.at[PRODUCTS, part], handed_vector.at[part], 3 + part).wait_send()
    for part in range(count):
        out_copy(part).wait()


def keep_kernel(updated_ref, handed_ref, updated_out, handed_out, rest, rest_updated, load, store):
    loads = [pltpu.make_async_copy(updated_ref, rest_updated, load.at[0])]
    stores = [pltpu.make_async_copy(rest_updated, updated_out, store.at[0])]
    for term in range(handed_ref.shape[2]):
        loads.append(pltpu.make_async_copy(handed_ref.at[0, 0, term], rest.at[term], load.at[term + 1]))
        stores.append(pltpu.make_async_copy(rest.at[term], handed_out.at[0, 0, term], store.at[term + 1]))
    for copy in loads:
        copy.start()
    for first, second in zip(loads, stores):
        first.wait()
        second.start()
    for copy in stores:
        copy.wait()


def keep(updated, handed):
    anywhere = pl.BlockSpec(memory_space=pl.ANY)
    copies = handed.shape[2] + 1
    return pl.pallas_call(
        keep_kernel,
        out_shape=(
            jax.ShapeDtypeStruct(updated.shape, BF16),
            jax.ShapeDtypeStruct(handed.shape, BF16),
        ),
        in_specs=[anywhere, anywhere],
        out_specs=(anywhere, anywhere),
        scratch_shapes=[
            pltpu.VMEM(handed.shape[2:], BF16),
            pltpu.VMEM(updated.shape, BF16),
            pltpu.SemaphoreType.DMA((copies,)),
            pltpu.SemaphoreType.DMA((copies,)),
        ],
        compiler_params=pltpu.CompilerParams(vmem_limit_bytes=60 * 2**20),
        name="keep",
    )(updated, handed)


def body(wavefunction, left_env, right_env, source, block_sizes, davidson_mix, ritz_weights):
    terms, width = left_env.shape[2], left_env.shape[3]
    count = width // LANES
    blocks = (terms, width, width)
    vmem, smem, anywhere = (pl.BlockSpec(memory_space=space) for space in (pltpu.VMEM, pltpu.SMEM, pl.ANY))
    tile = (8, LANES)
    norms = PRODUCTS + 2
    scratch = [pltpu.VMEM((RING * RING, width, LANES), BF16) for _ in range(2 * count)] + [
        pltpu.VMEM(blocks, BF16),
        pltpu.VMEM(blocks, BF16),
        pltpu.VMEM((count, terms * LANES, width), BF16),
        pltpu.VMEM(blocks, BF16),
        pltpu.VMEM((width, terms * LANES), BF16),
        pltpu.VMEM((width, width), F32),
        pltpu.VMEM((PRODUCTS + 1, count, width, LANES), BF16),
        pltpu.VMEM((width, width), F32),
        pltpu.VMEM((count, width, LANES), BF16),
        pltpu.VMEM((width, width), BF16),
        pltpu.VMEM((norms,) + tile, F32),
        pltpu.VMEM((norms, RING - 1) + tile, F32),
        pltpu.VMEM((norms,) + tile, F32),
        pltpu.VMEM((norms, RING - 1) + tile, F32),
        pltpu.VMEM((norms,) + tile, F32),
        pltpu.VMEM(tile, F32),
        pltpu.VMEM(tile, jnp.int32),
        pltpu.VMEM(tile, jnp.int32),
        pltpu.SMEM(tile, jnp.int32),
        pltpu.VMEM(davidson_mix.shape, F32),
        pltpu.SemaphoreType.DMA((3,)),
        pltpu.SemaphoreType.DMA((2, count)),
        pltpu.SemaphoreType.DMA((2, count, 2, 20)),
        pltpu.SemaphoreType.DMA((norms, 2, RING - 1)),
        pltpu.SemaphoreType.DMA((norms, 2, RING - 1)),
        pltpu.SemaphoreType.DMA((3 + count,)),
        pltpu.SemaphoreType.DMA((3 + count,)),
        pltpu.SemaphoreType.DMA,
        pltpu.SemaphoreType.DMA((count,)),
        pltpu.SemaphoreType.REGULAR,
    ]
    flops = (PRODUCTS + 1) * 2 * terms * 2 * width**3
    updated, handed = pl.pallas_call(
        kernel,
        out_shape=(
            jax.ShapeDtypeStruct(wavefunction.shape, BF16),
            jax.ShapeDtypeStruct(left_env.shape, BF16),
        ),
        in_specs=[vmem, anywhere, anywhere, smem, smem, anywhere, smem],
        out_specs=(vmem, anywhere),
        scratch_shapes=scratch,
        compiler_params=pltpu.CompilerParams(
            collective_id=0, has_side_effects=True, vmem_limit_bytes=60 * 2**20
        ),
        cost_estimate=pl.CostEstimate(flops=flops, bytes_accessed=40 * 2**20, transcendentals=0),
        name="davidson_update",
    )(wavefunction, left_env, right_env, source, block_sizes, davidson_mix, ritz_weights)
    return keep(updated, handed)


def solution(mesh):
    in_specs = (
        P("chain", "bond", None, None),
        P("chain", "bond", None, None, None),
        P("chain", "bond", None, None, None),
        P("chain", "bond", None),
        P("chain", "bond"),
        P("chain", None, None),
        P("chain", None),
    )
    out_specs = (P("chain", "bond", None, None), P("chain", "bond", None, None, None))
    return jax.shard_map(body, mesh=mesh, in_specs=in_specs, out_specs=out_specs, check_vma=False)
```

profile of v0, /device:TPU:0, one launch (start us, length us, event | category | flops | bytes accessed | tf_op | source)
XLA Modules:
  0.0 221.7 jit_solution(1322854706334228321)
XLA Ops:
  1.3 1.3 copy.9.mixing_hbm
  2.5 213.3 %davidson_update.1 = (bf16[1,1,512,512]{3,2,1,0:T(8,128)(2,1)}, bf16[1,1,12,512,512]{4,3,2,1,0:T(8,128)(2,1)}) custom-call(bf16[1,1,512,512]{3,2,1,0:T(8,128)(2,1)} %wave_ref.1, bf16[1,1,12,512,512]{4,3,2,1,0:T(8,128)(2,1)} %left_ref.1, bf16[1,1,12,512,512]{4,3,2,1,0:T(8,128)(2,1)} %right_ref.1, s32[1,1,12]{2,1,0:T(1,128)} %source_ref.1, ...), custom_call_target="tpu_custom_call" | custom-call | flops 25769803776 | bytes 41943040 | tf_op jit(solution)/shard_map/davidson_update/pallas_call | solution.py:547
  215.9 5.6 %keep.1 = (bf16[1,1,512,512]{3,2,1,0:T(8,128)(2,1)}, bf16[1,1,12,512,512]{4,3,2,1,0:T(8,128)(2,1)}) custom-call(bf16[1,1,512,512]{3,2,1,0:T(8,128)(2,1)} %get-tuple-element.4.updated_ref, bf16[1,1,12,512,512]{4,3,2,1,0:T(8,128)(2,1)} %get-tuple-element.5.handed_ref), custom_call_target="tpu_custom_call" | custom-call | tf_op jit(solution)/shard_map/keep/pallas_call | solution.py:488
where the time goes:
time: 222 us
  Pallas kernels  219 us (99%)
    pallas_call x1, Pallas kernels, body(): pl.pallas_call(kernel, out_shape=(jax.ShapeDtypeStruct(wavefunction.shape...  213 us
    pallas_call x1, Pallas kernels, keep(): pl.pallas_call(keep_kernel, out_shape=(jax.ShapeDtypeStruct(updated.shape...  5.64 us

commit v1 on v0

--- a/solution.py
+++ b/solution.py
@@ -17,10 +17,11 @@
 
 ORDER = (
     (("E", 1, 0), ("E", 1, 1), ("E", 2, 0), ("E", 1, 2), ("E", 3, 0), ("E", 2, 1), ("E", 1, 3), ("E", 4, 0))
-    + (("C", 0, 0), ("E", 3, 1), ("C", 0, 1), ("E", 2, 2), ("C", 0, 2), ("E", 4, 1), ("C", 0, 3), ("S", 0))
-    + (("E", 3, 2), ("C", 1, 0), ("C", 1, 1), ("E", 2, 3), ("C", 1, 2), ("C", 1, 3), ("S", 1), ("E", 4, 2))
-    + (("C", 2, 0), ("E", 3, 3), ("C", 2, 1), ("C", 2, 2), ("C", 2, 3), ("S", 2), ("E", 4, 3))
+    + (("C", 0, 0), ("E", 3, 1), ("C", 0, 1), ("E", 2, 2), ("C", 0, 2), ("E", 4, 1), ("S", 0))
+    + (("E", 3, 2), ("C", 1, 0), ("E", 2, 3), ("C", 1, 1), ("C", 1, 2), ("S", 1), ("E", 4, 2))
+    + (("C", 2, 0), ("E", 3, 3), ("C", 2, 1), ("C", 2, 2), ("S", 2), ("E", 4, 3))
 )
+GROUPS = 3
 EARLY = (("E", 1, 0), ("E", 1, 1), ("E", 2, 0), ("E", 1, 2))
 
 TURN = ("E", 4, 0)
@@ -146,7 +147,8 @@
 ):
     terms, width = left_ref.shape[2], left_ref.shape[3]
     count = width // LANES
-    group = terms // 4
+    group = terms // GROUPS
+    share = terms // len(EARLY)
     parts = (scratch[:count], scratch[count : 2 * count])
     (
         left,
@@ -309,7 +311,7 @@
                 turned[part, rows, :] = jnp.transpose(right[term, :, columns(part)])
             return carry
 
-        lax.fori_loop(number * group, (number + 1) * group, step, 0)
+        lax.fori_loop(number * share, (number + 1) * share, step, 0)
 
     def halves(number, part, which):
         held = parts[number % 2][part]
@@ -320,7 +322,7 @@
             half[:, pl.ds(pl.multiple_of(term * LANES, LANES), LANES)] = product.astype(BF16)
             return carry
 
-        lax.fori_loop(which * group, (which + 1) * group, step, 0, unroll=part == count - 1)
+        lax.fori_loop(which * group, (which + 1) * group, step, 0, unroll=group if part == count - 1 else 2)
 
     def gather_sum(part, side):
         wide = pl.ds(side * (width // 2), width // 2)
@@ -357,7 +359,7 @@
                 for side in (0, 1):
                     gather_sum(item[1], side)
         scales.append(norm_end(number))
-        for which in range(4):
+        for which in range(GROUPS):
             halves(number, count - 1, which)
         for part in range(count):
             here.sent(part)
@@ -410,7 +412,7 @@
             right[term] = product.astype(BF16)
             return carry
 
-        lax.fori_loop(which * group, (which + 1) * group, step, 0)
+        lax.fori_loop(which * share, (which + 1) * share, step, 0)
 
     def out_copy(part):
         return pltpu.make_async_copy(
@@ -426,7 +428,7 @@
             left[term, :, columns(part)] = (product * factor).astype(BF16)
             return carry
 
-        lax.fori_loop(which * group, (which + 1) * group, step, 0, unroll=part == count - 1)
+        lax.fori_loop(which * group, (which + 1) * group, step, 0, unroll=group if part == count - 1 else 2)
 
     factor = None
     for item in ORDER:
@@ -449,7 +451,7 @@
             grow(*item[1:], factor)
         else:
             out_copy(item[1]).start()
-    for which in range(4):
+    for which in range(GROUPS):
         grow(count - 1, which, factor)
     out_copy(count - 1).start()
     for part in range(count):

time: 222 us -> 219 us (0.986)
  Pallas kernels: 219 us -> 216 us
    pallas_call x1, Pallas kernels: 213 us -> 210 us  [body(): pl.pallas_call(kernel, out_shape=(jax.ShapeDtypeStruct(wavefunction.shape...]
where the time goes in v1:
time: 219 us
  Pallas kernels  216 us (99%)
    pallas_call x1, Pallas kernels, body(): pl.pallas_call(kernel, out_shape=(jax.ShapeDtypeStruct(wavefunction.shape...  210 us
    pallas_call x1, Pallas kernels, keep(): pl.pallas_call(keep_kernel, out_shape=(jax.ShapeDtypeStruct(updated.shape...  5.64 us

profile of v1, /device:TPU:0, one launch (start us, length us, event | category | flops | bytes accessed | tf_op | source)
XLA Modules:
  0.0 218.6 jit_solution(8191238456733151543)
XLA Ops:
  1.3 1.3 copy.9.mixing_hbm
  2.5 210.2 %davidson_update.1 = (bf16[1,1,512,512]{3,2,1,0:T(8,128)(2,1)}, bf16[1,1,12,512,512]{4,3,2,1,0:T(8,128)(2,1)}) custom-call(bf16[1,1,512,512]{3,2,1,0:T(8,128)(2,1)} %wave_ref.1, bf16[1,1,12,512,512]{4,3,2,1,0:T(8,128)(2,1)} %left_ref.1, bf16[1,1,12,512,512]{4,3,2,1,0:T(8,128)(2,1)} %right_ref.1, s32[1,1,12]{2,1,0:T(1,128)} %source_ref.1, ...), custom_call_target="tpu_custom_call" | custom-call | flops 25769803776 | bytes 41943040 | tf_op jit(solution)/shard_map/davidson_update/pallas_call | solution.py:549
  212.8 5.6 %keep.1 = (bf16[1,1,512,512]{3,2,1,0:T(8,128)(2,1)}, bf16[1,1,12,512,512]{4,3,2,1,0:T(8,128)(2,1)}) custom-call(bf16[1,1,512,512]{3,2,1,0:T(8,128)(2,1)} %get-tuple-element.4.updated_ref, bf16[1,1,12,512,512]{4,3,2,1,0:T(8,128)(2,1)} %get-tuple-element.5.handed_ref), custom_call_target="tpu_custom_call" | custom-call | tf_op jit(solution)/shard_map/keep/pallas_call | solution.py:490
